TPU v7x, 256 devices: a whole 4x4x8 slice. The times are simulated.
256 devices in a mesh: dp: 32 (over y, z_hi, core), node: 8 (over z_lo, x).
Axes of the slice: x: 4, y: 4, z: 8 (z_hi: 4, z_lo: 2; z = z_hi * 2 + z_lo), core: 2. Of those that a mesh axis runs over, the one named last changes fastest.
Arguments:
- tokens: bfloat16 [65536, 4096], P(('dp', 'node')), may hold values from -6 to 6
- cotangent: bfloat16 [65536, 1024], P(('dp', 'node')), may hold values from -6 to 6
- quantized: bfloat16 [4096, 1024], P('dp'), may hold values from -127 to 127, as said below
- scales: float32 [4096, 4], P('dp'), may hold values from 0.0001 to 0.0004
Outputs:
- keys: bfloat16 [65536, 1024], P(('dp', 'node'))
- grad_input: bfloat16 [65536, 4096], P(('dp', 'node'))
- grad_weight: float32 [4096, 1024], P('dp', 'node')
Inputs may be any that keep to these rules, and one draw needn't show every extreme that they name: `quantized`: whole numbers.
All inputs are finite; a program needn't handle non-finite values.
Results may differ from a plain program's by a relative error of at most 0.005.
Values may be sent and summed in bfloat16 or wider, within the bound.
A program may use at most 128 MiB of HBM per device.

v0:
```python
import jax
import jax.numpy as jnp
from jax import lax
from jax.sharding import PartitionSpec as P


def shards(tokens, cotangent, quantized, scales):
    local_rows = quantized.shape[0]
    groups = scales.shape[1]
    width = quantized.shape[1]
    codes = quantized.astype(jnp.float32).reshape(local_rows, groups, width // groups)
    local_weight = (codes * scales[:, :, None]).reshape(local_rows, width).astype(jnp.bfloat16)
    weight = lax.all_gather(local_weight, "dp", axis=0, tiled=True)
    keys = jnp.dot(tokens, weight, preferred_element_type=jnp.float32).astype(jnp.bfloat16)
    grad_input = lax.dot_general(
        cotangent, weight, (((1,), (1,)), ((), ())), preferred_element_type=jnp.float32
    ).astype(jnp.bfloat16)
    partial_value = lax.dot_general(
        tokens, cotangent, (((0,), (0,)), ((), ())), preferred_element_type=jnp.float32
    )
    node_sums = lax.psum_scatter(partial_value, "node", scatter_dimension=1, tiled=True)
    owned = lax.psum_scatter(node_sums, "dp", scatter_dimension=0, tiled=True)
    total_tokens = tokens.shape[0] * lax.axis_size("dp") * lax.axis_size("node")
    grad_weight = owned * float(total_tokens) ** (-0.5)
    return (keys, grad_input, grad_weight)


def solution(mesh):
    in_specs = (P(("dp", "node"), None), P(("dp", "node"), None), P("dp", None), P("dp", None))
    out_specs = (P(("dp", "node"), None), P(("dp", "node"), None), P("dp", "node"))
    return jax.shard_map(shards, mesh=mesh, in_specs=in_specs, out_specs=out_specs, check_vma=False)
```

profile of v0, /device:TPU:8, one launch (start us, length us, event | category | flops | bytes accessed | tf_op | source)
XLA Modules:
  0.0 336.0 jit_solution(8663128587629536193)
XLA Ops:
  8.0 0.0 copy-start
  8.0 0.0 reduce-scatter.3.cloned.1.call-start
  8.1 1.5 copy-done
  9.6 9.2 %fusion.2 = f32[4096,1024]{1,0:T(8,128)} fusion(bf16[256,4096]{1,0:T(8,128)(2,1)S(1)} %copy-done, bf16[256,1024]{1,0:T(8,128)(2,1)} %param.5), kind=kOutput, calls=%fused_computation.6 | convolution fusion | flops 2147483648 | bytes 19398656 | tf_op jit(solution)/shard_map/dot_general | solution.py:18
  18.7 0.0 copy-start.3
  18.8 0.0 copy-start.2
  18.8 0.0 reduce-scatter.3.cloned.1.call-update
  18.8 0.0 all-gather.2.cloned.1.call-start
  18.8 0.6 copy-done.3
  19.4 0.1 copy.7
  19.5 0.2 mul.17
  19.7 0.0 copy-start.1
  19.8 0.1 copy.10
  19.9 0.0 copy-done.2
  19.9 0.8 multiply_convert_fusion
  20.6 0.0 all-gather.2.cloned.1.call-update
  20.7 0.0 reduce-scatter.5.cloned.1.call-start
  20.7 217.1 %reduce-scatter.3.cloned.1.call-done = f32[4096,128]{1,0:T(8,128)} async-done(((f32[4096,1024]{1,0:T(8,128)}), f32[4096,128]{1,0:T(8,128)}) %reduce-scatter.3.cloned.1.call-update) | async-done | bytes 2097168 | tf_op jit(solution)/shard_map/reduce_scatter | solution.py:21
  237.9 0.0 reduce-scatter.5.cloned.1.call-update
  237.9 0.0 all-gather.2.cloned.1.call-done
  237.9 0.0 copy-done.1
  237.9 7.1 %fusion = bf16[256,4096]{0,1:T(8,128)(2,1)} fusion(bf16[4096,1024]{1,0:T(8,128)(2,1)} %all-gather.2.cloned.1.call-done, bf16[256,1024]{1,0:T(8,128)(2,1)S(1)} %copy-done.1), kind=kOutput, calls=%fused_computation.1 | convolution fusion | flops 2148532224 | bytes 11010048 | tf_op jit(solution)/shard_map/dot_general | solution.py:15
  245.0 4.1 %copy.9 = bf16[256,4096]{1,0:T(8,128)(2,1)} copy(bf16[256,4096]{0,1:T(8,128)(2,1)} %fusion) | data formatting | bytes 4194304
  249.1 5.9 %fusion.1 = bf16[256,1024]{0,1:T(8,128)(2,1)S(1)} fusion(bf16[4096,1024]{1,0:T(8,128)(2,1)} %all-gather.2.cloned.1.call-done, bf16[256,4096]{1,0:T(8,128)(2,1)S(1)} %copy-done), kind=kOutput, calls=%fused_computation.3 | convolution fusion | flops 2147745792 | bytes 11010048 | tf_op jit(solution)/shard_map/dot_general | solution.py:14
  255.0 1.0 copy.8
  256.0 71.1 %reduce-scatter.5.cloned.1.call-done = f32[128,128]{1,0:T(8,128)} async-done(((f32[4096,128]{1,0:T(8,128)}), f32[128,128]{1,0:T(8,128)}) %reduce-scatter.5.cloned.1.call-update) | async-done | bytes 65552 | tf_op jit(solution)/shard_map/reduce_scatter | solution.py:22
  327.1 1.5 broadcast_multiply_fusion
Async XLA Ops:
  8.0 1.6 copy-start
  8.0 229.8 %reduce-scatter.3.cloned.1.call-start = ((), (), s32[]{:S(2)}) async-start(), calls=%async_computation.3 | async-start | bytes 18874368 | tf_op jit(solution)/shard_map/reduce_scatter | solution.py:21
  18.7 0.7 copy-start.3
  18.8 1.1 copy-start.2
  18.8 219.1 %all-gather.2.cloned.1.call-start = ((), (), s32[]{:S(2)}) async-start(), calls=%async_computation.2 | async-start | bytes 8650752 | tf_op jit(solution)/shard_map/all_gather | solution.py:13
  19.7 218.2 %copy-start.1 = (bf16[256,1024]{1,0:T(8,128)(2,1)S(1)}, bf16[256,1024]{1,0:T(8,128)(2,1)}, u32[]{:S(2)}) copy-start(bf16[256,1024]{1,0:T(8,128)(2,1)} %param.5) | copy-start | bytes 1572868
  20.7 306.4 %reduce-scatter.5.cloned.1.call-start = ((), (), s32[]{:S(2)}) async-start(), calls=%async_computation.4 | async-start | bytes 2162688 | tf_op jit(solution)/shard_map/reduce_scatter | solution.py:22
Sparse Core Ops, SparseCore 0:
  18.9 218.9 reduce-scatter.2
Sparse Core Ops, SparseCore 1:
  22.4 135.1 all-gather.1
  238.0 89.1 reduce-scatter.4
where the time goes:
time: 337 us; the launch traced here: 336 us
  waiting for transfers between devices  288 us (85%)
  matrix products  22.2 us (7%)
  between operations  15.5 us (5%)
  local copies, waits for them, and re-layouts  7.64 us (2%)
    reduce_scatter x1, waiting for transfers between devices, shards(): lax.psum_scatter(partial_value, 'node', scatter_dimension=1, tiled=True)  217 us
    reduce_scatter x1, waiting for transfers between devices, shards(): owned = lax.psum_scatter(node_sums, 'dp', scatter_dimension=0, tiled=True)  71.1 us
    dot_general x1, matrix products, shards(): lax.dot_general(tokens, cotangent, (((0,), (0,)), ((), ())), preferred_el...  9.16 us
    unnamed x12, local copies, waits for them, and re-layouts  7.44 us
    dot_general x1, matrix products, shards(): lax.dot_general(cotangent, weight, (((1,), (1,)), ((), ())), preferred_el...  7.11 us
  transfers between devices with their start and end apart: 3, of which 2 were waited for; matrix products, arithmetic and copies ran while one was open for 6% of the time, Pallas kernels for 0%

commit v1 on v0

v1 whole, which is shorter than its diff:
```python
import jax
import jax.numpy as jnp
from jax import lax
from jax.experimental import pallas as pl
from jax.experimental.pallas import tpu as pltpu
from jax.sharding import PartitionSpec as P

MESH = pl.DeviceIdType.MESH
BF = jnp.bfloat16
F32 = jnp.float32


def nn(a, b):
    return lax.dot_general(a, b, (((1,), (0,)), ((), ())), preferred_element_type=F32)


def nt(a, b):
    return lax.dot_general(a, b, (((1,), (1,)), ((), ())), preferred_element_type=F32)


def kernel(
    tok, cot, quantized, scales_t, keys_o, gi_o, gw_o,
    tk, ct, ctt, w1, w2, s1s, s1r, dps, dpr, s2s, s2r, xo, ys, yr, yt, zs, zr, kacc, krecv, kout, gis,
    tok_l, tok_s, tok_r, cot_l, cot_s, cot_r, key_s, key_r, key_l, gi_l, gi_s, gi_r,
    hy_s, hy_r, hz1_s, hz1_r, hz2_s, hz2_r, gz1_s, gz1_r, gz2_s, gz2_r, gy_s, gy_r,
    s1_s, s1_q, dp_s, dp_q, s2_s, s2_q, y_s, y_q, z_s, z_q,
):
    dp, node = lax.axis_index("dp"), lax.axis_index("node")
    y, zh, c = dp // 8, (dp // 2) % 4, dp % 2
    zl, x = node // 4, node % 4
    z = zh * 2 + zl
    dirz = 2 * zl - 1

    def at(dx=0, dy=0, dz=0, dc=0):
        x2, y2, z2 = (x + dx + 4) % 4, (y + dy + 4) % 4, (z + dz + 8) % 8
        c2 = c if dc == 0 else 1 - c
        return (y2 * 8 + (z2 // 2) * 2 + c2, (z2 % 2) * 4 + x2)

    sib = at(dc=1)
    pair = at(dz=0 - dirz)
    pending = []

    def send(src, dst, ss, rs, dev):
        cp = pltpu.make_async_remote_copy(src, dst, ss, rs, device_id=dev, device_id_type=MESH)
        cp.start()
        pending.append(cp)

    def arrived(dst, rs):
        pltpu.make_async_remote_copy(dst, dst, rs, rs, device_id=sib, device_id_type=MESH).wait_recv()

    def mod4(v):
        return (v + 4) % 4

    def cols(yy, h):
        return pl.ds(pl.multiple_of(((yy * 4 + h) * 2 + c) * 128, 128), 128)

    def cols_sib(yy, h):
        return pl.ds(pl.multiple_of(((yy * 4 + h) * 2 + 1 - c) * 128, 128), 128)

    cp_cot = pltpu.make_async_copy(cot, ct.at[pl.ds(0, 256)], cot_l)
    cp_cot.start()
    for i in range(4):
        yy = (y + i + 1) % 4
        for h in range(4):
            pltpu.make_async_copy(
                tok.at[:, cols(yy, h)], tk.at[yy, pl.ds(0, 256), pl.ds(h * 128, 128)], tok_l.at[i]
            ).start()

    for b in range(4):
        scale = jnp.transpose(jnp.broadcast_to(scales_t[b : b + 1, :], (128, 128)))
        for half in range(2):
            col = b * 256 + half * 128
            block = (quantized[:, col : col + 128].astype(F32) * scale).astype(BF)
            if col < 512:
                w1[y, zh, :, col : col + 128] = block
            else:
                w2[y, zh, :, col - 512 : col - 384] = block

    barrier = pltpu.get_barrier_semaphore()
    peers = [at(dx=1), at(dx=-1)] + [at(dy=o) for o in (1, 2, 3)] + [at(dz=j) for j in range(1, 8)] + [sib]
    for peer in peers:
        pl.semaphore_signal(barrier, inc=1, device_id=peer, device_id_type=MESH)
    pl.semaphore_wait(barrier, len(peers))

    send(cot, ct.at[pl.ds(256, 256)], cot_s, cot_r, sib)
    for i in range(4):
        yy = (y + i + 1) % 4
        for h in range(4):
            pltpu.make_async_remote_copy(
                tok.at[:, cols_sib(yy, h)], tk.at[yy, pl.ds(256, 256), pl.ds(h * 128, 128)],
                tok_s.at[i], tok_r.at[i], device_id=sib, device_id_type=MESH,
            ).start()

    def half(flag):
        return pl.ds(pl.multiple_of(flag * 64, 64), 64)

    def z1(w, yy, ss, rs):
        send(w.at[yy, zh], w.at[yy, zh], ss.at[0], rs.at[0], at(dz=dirz))
        send(w.at[yy, zh, half(1 - zl)], w.at[yy, zh, half(1 - zl)], ss.at[1], rs.at[1], at(dz=3 * dirz))

    def z1_arrived(w, yy, rs):
        arrived(w.at[yy, mod4(zh + dirz)], rs.at[0])
        arrived(w.at[yy, mod4(zh + 2), half(zl)], rs.at[1])

    def z2(w, yy, ss, rs):
        near, far = mod4(zh + dirz), mod4(zh + 2)
        send(w.at[yy, near], w.at[yy, near], ss.at[0], rs.at[0], pair)
        send(w.at[yy, far, half(zl)], w.at[yy, far, half(zl)], ss.at[1], rs.at[1], pair)

    def z2_arrived(w, yy, rs):
        arrived(w.at[yy, mod4(zh - dirz)], rs.at[0])
        arrived(w.at[yy, mod4(zh + 2), half(1 - zl)], rs.at[1])

    def w2_along_y(zz, role):
        for o in (1, 3, 2):
            send(w2.at[y, zz], w2.at[y, zz], gy_s.at[role, o - 1], gy_r.at[role, o - 1], at(dy=o))

    z1(w2, y, gz1_s, gz1_r)
    for o in (1, 3, 2):
        send(w1.at[y, zh], w1.at[y, zh], hy_s.at[o - 1], hy_r.at[o - 1], at(dy=o))
    z1(w1, y, hz1_s.at[0], hz1_r.at[0])
    w2_along_y(zh, 0)

    def transpose_rows(r):
        for n in range(8):
            part = ct[r * 256 : r * 256 + 256, n * 128 : n * 128 + 128]
            row = (n // 4) * 128
            ctt[n % 4, row : row + 128, r * 256 : r * 256 + 256] = jnp.transpose(part)

    cp_cot.wait()
    transpose_rows(0)
    arrived(ct.at[pl.ds(256, 256)], cot_r)
    transpose_rows(1)

    east, west = at(dx=1), at(dx=-1)
    lo, hi = pl.ds(0, 128), pl.ds(128, 128)
    xe, xw, xf = (x + 1) % 4, (x + 3) % 4, (x + 2) % 4

    for i in range(4):
        yy = (y + i + 1) % 4
        pltpu.make_async_copy(tk.at[yy, pl.ds(0, 256)], tk.at[yy, pl.ds(0, 256)], tok_l.at[i]).wait()
        arrived(tk.at[yy, pl.ds(256, 256)], tok_r.at[i])
        s1s[i] = nn(ctt[xf], tk[yy]).astype(BF)
        send(s1s.at[i, lo], s1r.at[i, lo], s1_s.at[i, 0], s1_q.at[i, 0], east)
        send(s1s.at[i, hi], s1r.at[i, hi], s1_s.at[i, 1], s1_q.at[i, 1], west)

    def x_step(i):
        yy = (y + i + 1) % 4
        right, left = nn(ctt[xe], tk[yy]), nn(ctt[xw], tk[yy])
        dps[i, 128:256] = right[128:256].astype(BF)
        dps[i, 0:128] = left[0:128].astype(BF)
        send(dps.at[i, hi], dpr.at[i, hi], dp_s.at[i, 1], dp_q.at[i, 1], east)
        send(dps.at[i, lo], dpr.at[i, lo], dp_s.at[i, 0], dp_q.at[i, 0], west)
        arrived(s1r.at[i, lo], s1_q.at[i, 0])
        s2s[i, 0:128] = (right[0:128] + s1r[i, 0:128].astype(F32)).astype(BF)
        send(s2s.at[i, lo], s2r.at[i, lo], s2_s.at[i, 0], s2_q.at[i, 0], east)
        arrived(s1r.at[i, hi], s1_q.at[i, 1])
        s2s[i, 128:256] = (left[128:256] + s1r[i, 128:256].astype(F32)).astype(BF)
        send(s2s.at[i, hi], s2r.at[i, hi], s2_s.at[i, 1], s2_q.at[i, 1], west)

    def x_end(i):
        yy = (y + i + 1) % 4
        total = nn(ctt[x], tk[yy])
        for k, rows in ((0, lo), (1, hi)):
            arrived(dpr.at[i, rows], dp_q.at[i, k])
            arrived(s2r.at[i, rows], s2_q.at[i, k])
        total = total + dpr[i].astype(F32) + s2r[i].astype(F32)
        if i < 3:
            ys[i] = total.astype(BF)
            send(ys.at[i], yr.at[i], y_s.at[i], y_q.at[i], at(dy=i + 1))
        else:
            xo[...] = total

    z1_arrived(w2, y, gz1_r)
    z2(w2, y, gz2_s, gz2_r)
    w2_along_y(mod4(zh + dirz), 1)
    for o in (1, 3, 2):
        yy = mod4(y - o)
        arrived(w1.at[yy, zh], hy_r.at[o - 1])
        z1(w1, yy, hz1_s.at[4 - o], hz1_r.at[4 - o])
    x_step(0)
    z2_arrived(w2, y, gz2_r)
    w2_along_y(mod4(zh - dirz), 2)
    w2_along_y(mod4(zh + 2), 3)
    z1_arrived(w1, y, hz1_r.at[0])
    z2(w1, y, hz2_s.at[0], hz2_r.at[0])
    x_step(1)
    for o in (1, 3):
        yy = mod4(y - o)
        z1_arrived(w1, yy, hz1_r.at[4 - o])
        z2(w1, yy, hz2_s.at[4 - o], hz2_r.at[4 - o])
    x_step(2)
    yy = mod4(y - 2)
    z1_arrived(w1, yy, hz1_r.at[2])
    z2(w1, yy, hz2_s.at[2], hz2_r.at[2])
    x_step(3)
    x_end(0)

    for r in range(4):
        z2_arrived(w1, (y + r) % 4, hz2_r.at[r])
    roles = (zh, mod4(zh + dirz), mod4(zh - dirz), mod4(zh + 2))
    for role in range(4):
        for o in (1, 3, 2):
            arrived(w2.at[mod4(y - o), roles[role]], gy_r.at[role, o - 1])

    def use_weight(p):
        a, b = w1[p].reshape(512, 512), w2[p].reshape(512, 512)
        for r in range(2):
            rows = slice(r * 256, r * 256 + 256)
            gis[p, rows] = (nt(ct[rows, 0:512], a) + nt(ct[rows, 512:1024], b)).astype(BF)
        for h in range(4):
            here = pl.ds(h * 128, 128)
            pltpu.make_async_remote_copy(
                gis.at[p, pl.ds(256, 256), here], gi_o.at[:, cols(p, h)],
                gi_s, gi_r, device_id=sib, device_id_type=MESH,
            ).start()
            pltpu.make_async_copy(gis.at[p, pl.ds(0, 256), here], gi_o.at[:, cols(p, h)], gi_l).start()
        if p == 0:
            kacc[:, 0:512] = nn(tk[p], a)
            kacc[:, 512:1024] = nn(tk[p], b)
        else:
            kacc[:, 0:512] += nn(tk[p], a)
            kacc[:, 512:1024] += nn(tk[p], b)

    use_weight(0)
    x_end(1)
    use_weight(1)
    x_end(2)
    use_weight(2)
    x_end(3)
    for i in range(3):
        arrived(yr.at[i], y_q.at[i])
    total = xo[...] + yr[0].astype(F32) + yr[1].astype(F32) + yr[2].astype(F32)
    for b in range(8):
        block = total[(b % 2) * 128 : (b % 2) * 128 + 128, (b // 2) * 128 : (b // 2) * 128 + 128]
        yt[b] = block
        zs[b] = block.astype(BF)
    for j in (4, 3, 5, 2, 6, 1, 7):
        send(zs.at[(z + j) % 8], zr.at[j - 1], z_s.at[j - 1], z_q.at[j - 1], at(dz=j))
    use_weight(3)
    send(kacc.at[pl.ds(256, 256)], krecv, key_s, key_r, sib)
    for j in (1, 7, 2, 6, 3, 5, 4):
        arrived(zr.at[j - 1], z_q.at[j - 1])
    acc = yt[z]
    for j in range(7):
        acc = acc + zr[j].astype(F32)
    gw_o[...] = jnp.transpose(acc) * 0.00390625
    arrived(krecv, key_r)
    kout[...] = (kacc[0:256] + krecv[...]).astype(BF)
    cp_key = pltpu.make_async_copy(kout, keys_o, key_l)
    cp_key.start()

    for cp in pending:
        cp.wait_send()
    for i in range(4):
        pltpu.make_async_copy(tk.at[0, pl.ds(256, 256)], tk.at[0, pl.ds(256, 256)], tok_s.at[i]).wait()
    wide = pl.ds(0, 2048)
    pltpu.make_async_copy(gi_o.at[:, wide], gi_o.at[:, wide], gi_l).wait()
    pltpu.make_async_copy(gi_o.at[:, wide], gi_o.at[:, wide], gi_s).wait()
    pltpu.make_async_copy(gi_o.at[:, wide], gi_o.at[:, wide], gi_r).wait()
    cp_key.wait()


def shards(tokens, cotangent, quantized, scales):
    dma = pltpu.SemaphoreType.DMA
    vm = pltpu.VMEM
    piece = (4, 256, 512)
    scratch = [
        vm((4, 512, 512), BF), vm((512, 1024), BF), vm((4, 256, 512), BF),
        vm((4, 4, 128, 512), BF), vm((4, 4, 128, 512), BF),
        vm(piece, BF), vm(piece, BF), vm(piece, BF), vm(piece, BF), vm(piece, BF), vm(piece, BF),
        vm((256, 512), F32), vm((3, 256, 512), BF), vm((3, 256, 512), BF),
        vm((8, 128, 128), F32), vm((8, 128, 128), BF), vm((7, 128, 128), BF),
        vm((512, 1024), F32), vm((256, 1024), F32), vm((256, 1024), BF), vm((4, 512, 512), BF),
        dma((4,)), dma((4,)), dma((4,)), dma, dma, dma, dma, dma, dma, dma, dma, dma,
        dma((3,)), dma((3,)), dma((4, 2)), dma((4, 2)), dma((4, 2)), dma((4, 2)),
        dma((2,)), dma((2,)), dma((2,)), dma((2,)), dma((4, 3)), dma((4, 3)),
        dma((4, 2)), dma((4, 2)), dma((4, 2)), dma((4, 2)), dma((4, 2)), dma((4, 2)),
        dma((3,)), dma((3,)), dma((7,)), dma((7,)),
    ]
    anywhere = pl.BlockSpec(memory_space=pl.ANY)
    vmem = pl.BlockSpec(memory_space=pltpu.VMEM)
    return pl.pallas_call(
        kernel,
        out_shape=(
            jax.ShapeDtypeStruct((256, 1024), BF),
            jax.ShapeDtypeStruct((256, 4096), BF),
            jax.ShapeDtypeStruct((128, 128), F32),
        ),
        in_specs=[anywhere, anywhere, vmem, vmem],
        out_specs=(anywhere, anywhere, vmem),
        scratch_shapes=scratch,
        compiler_params=pltpu.CompilerParams(
            collective_id=0, has_side_effects=True, vmem_limit_bytes=48 * 2**20
        ),
        cost_estimate=pl.CostEstimate(flops=6442450944, bytes_accessed=8 * 2**20, transcendentals=0),
        name="key_projection",
    )(tokens, cotangent, quantized, scales.T)


def solution(mesh):
    in_specs = (P(("dp", "node"), None), P(("dp", "node"), None), P("dp", None), P("dp", None))
    out_specs = (P(("dp", "node"), None), P(("dp", "node"), None), P("dp", "node"))
    return jax.shard_map(shards, mesh=mesh, in_specs=in_specs, out_specs=out_specs, check_vma=False)
```

time: 337 us -> 76.9 us (0.23)
  waiting for transfers between devices: 288 us -> 0 us
  Pallas kernels: 0 us -> 69.1 us
  matrix products: 22.2 us -> 0 us
  between operations: 15.5 us -> 0.65 us
    reduce_scatter x2 -> x0, waiting for transfers between devices: 288 us -> none  [the longest x1 217 us: shards(): lax.psum_scatter(partial_value, 'node', scatter_dimension=1, tiled=True)]
    pallas_call x0 -> x1, Pallas kernels: none -> 69.1 us  [shards(): pl.pallas_call(kernel, out_shape=(jax.ShapeDtypeStruct((256, 1024), BF),...]
    dot_general x3 -> x0, matrix products: 22.2 us -> none  [the longest x1 9.16 us: shards(): lax.dot_general(tokens, cotangent, (((0,), (0,)), ((), ())), preferred_el...]
    unnamed x12 -> x11, local copies, waits for them, and re-layouts: 7.44 us -> 7 us
  transfers between devices with their start and end apart: 3 -> 0, of which waited for: 2 -> 0; matrix products, arithmetic and copies ran while one was open for 6% -> 0% of each run, Pallas kernels for 0% -> 0%
where the time goes in v1:
time: 76.9 us; the launch traced here: 76.7 us
  Pallas kernels  69.1 us (90%)
  local copies, waits for them, and re-layouts  7 us (9%)
    pallas_call x1, Pallas kernels, shards(): pl.pallas_call(kernel, out_shape=(jax.ShapeDtypeStruct((256, 1024), BF),...  69.1 us
    unnamed x11, local copies, waits for them, and re-layouts  7 us

profile of v1, /device:TPU:8, one launch (start us, length us, event | category | flops | bytes accessed | tf_op | source)
XLA Modules:
  0.0 76.7 jit_solution(7459110190145018284)
XLA Ops:
  0.6 0.0 copy-start
  0.6 1.6 %copy-done = bf16[256,4096]{1,0:T(8,128)(2,1)S(1)} copy-done((bf16[256,4096]{1,0:T(8,128)(2,1)S(1)}, bf16[256,4096]{1,0:T(8,128)(2,1)}, u32[]{:S(2)}) %copy-start) | copy-done | bytes 2097176
  2.2 0.0 copy-start.1
  2.2 1.0 %copy-done.1 = bf16[256,1024]{1,0:T(8,128)(2,1)S(1)} copy-done((bf16[256,1024]{1,0:T(8,128)(2,1)S(1)}, bf16[256,1024]{1,0:T(8,128)(2,1)}, u32[]{:S(2)}) %copy-start.1) | copy-done | bytes 524312
  3.3 0.0 copy-start.2
  3.3 0.9 %copy-done.2 = bf16[128,1024]{1,0:T(8,128)(2,1)S(1)} copy-done((bf16[128,1024]{1,0:T(8,128)(2,1)S(1)}, bf16[128,1024]{1,0:T(8,128)(2,1)}, u32[]{:S(2)}) %copy-start.2) | copy-done | bytes 262168
  4.2 0.0 copy-start.3
  4.2 0.7 copy-done.3
  4.9 69.1 %key_projection.1 = (bf16[256,1024]{1,0:T(8,128)(2,1)S(1)}, bf16[256,4096]{1,0:T(8,128)(2,1)S(1)}, f32[128,128]{1,0:T(8,128)S(1)}) custom-call(bf16[256,4096]{1,0:T(8,128)(2,1)S(1)} %copy-done, bf16[256,1024]{1,0:T(8,128)(2,1)S(1)} %copy-done.1, bf16[128,1024]{1,0:T(8,128)(2,1)S(1)} %copy-done.2, f32[4,128]{1,0:T(4,128)S(1)} %bitcast.1), custom_call_target="tpu_custom_call" | custom-call | flops 6442450944 | bytes 8388608 | tf_op jit(solution)/shard_map/key_projection/pallas_call | solution.py:283
  74.0 0.8 %copy.10 = bf16[256,1024]{1,0:T(8,128)(2,1)} copy(bf16[256,1024]{1,0:T(8,128)(2,1)S(1)} %get-tuple-element.6) | data formatting | bytes 1048576
  74.8 1.3 %copy.11 = bf16[256,4096]{1,0:T(8,128)(2,1)} copy(bf16[256,4096]{1,0:T(8,128)(2,1)S(1)} %get-tuple-element.7) | data formatting | bytes 4194304
  76.1 0.6 copy.12
Async XLA Ops:
  0.6 1.6 %copy-start = (bf16[256,4096]{1,0:T(8,128)(2,1)S(1)}, bf16[256,4096]{1,0:T(8,128)(2,1)}, u32[]{:S(2)}) copy-start(bf16[256,4096]{1,0:T(8,128)(2,1)} %tok.1) | copy-start | bytes 6291460
  2.2 1.0 %copy-start.1 = (bf16[256,1024]{1,0:T(8,128)(2,1)S(1)}, bf16[256,1024]{1,0:T(8,128)(2,1)}, u32[]{:S(2)}) copy-start(bf16[256,1024]{1,0:T(8,128)(2,1)} %cot.1) | copy-start | bytes 1572868
  3.3 0.9 %copy-start.2 = (bf16[128,1024]{1,0:T(8,128)(2,1)S(1)}, bf16[128,1024]{1,0:T(8,128)(2,1)}, u32[]{:S(2)}) copy-start(bf16[128,1024]{1,0:T(8,128)(2,1)} %quantized.1) | copy-start | bytes 786436
  4.2 0.7 copy-start.3

commit v2 on v1

--- a/solution.py
+++ b/solution.py
@@ -22,7 +22,7 @@
     tok, cot, quantized, scales_t, keys_o, gi_o, gw_o,
     tk, ct, ctt, w1, w2, s1s, s1r, dps, dpr, s2s, s2r, xo, ys, yr, yt, zs, zr, kacc, krecv, kout, gis,
     tok_l, tok_s, tok_r, cot_l, cot_s, cot_r, key_s, key_r, key_l, gi_l, gi_s, gi_r,
-    hy_s, hy_r, hz1_s, hz1_r, hz2_s, hz2_r, gz1_s, gz1_r, gz2_s, gz2_r, gy_s, gy_r,
+    hy_s, hy_r, hz_s, hz_r, gz_s, gz_r, gy_s, gy_r,
     s1_s, s1_q, dp_s, dp_q, s2_s, s2_q, y_s, y_q, z_s, z_q,
 ):
     dp, node = lax.axis_index("dp"), lax.axis_index("node")
@@ -37,7 +37,6 @@
         return (y2 * 8 + (z2 // 2) * 2 + c2, (z2 % 2) * 4 + x2)
 
     sib = at(dc=1)
-    pair = at(dz=0 - dirz)
     pending = []
 
     def send(src, dst, ss, rs, dev):
@@ -94,32 +93,55 @@
     def half(flag):
         return pl.ds(pl.multiple_of(flag * 64, 64), 64)
 
-    def z1(w, yy, ss, rs):
-        send(w.at[yy, zh], w.at[yy, zh], ss.at[0], rs.at[0], at(dz=dirz))
-        send(w.at[yy, zh, half(1 - zl)], w.at[yy, zh, half(1 - zl)], ss.at[1], rs.at[1], at(dz=3 * dirz))
-
-    def z1_arrived(w, yy, rs):
-        arrived(w.at[yy, mod4(zh + dirz)], rs.at[0])
-        arrived(w.at[yy, mod4(zh + 2), half(zl)], rs.at[1])
-
-    def z2(w, yy, ss, rs):
-        near, far = mod4(zh + dirz), mod4(zh + 2)
-        send(w.at[yy, near], w.at[yy, near], ss.at[0], rs.at[0], pair)
-        send(w.at[yy, far, half(zl)], w.at[yy, far, half(zl)], ss.at[1], rs.at[1], pair)
-
-    def z2_arrived(w, yy, rs):
-        arrived(w.at[yy, mod4(zh - dirz)], rs.at[0])
-        arrived(w.at[yy, mod4(zh + 2), half(1 - zl)], rs.at[1])
-
-    def w2_along_y(zz, role):
+    cross, pair = at(dz=dirz), at(dz=0 - dirz)
+    near, back, far = mod4(zh + dirz), mod4(zh - dirz), mod4(zh + 2)
+
+    def z_send(w, yy, phase, ss, rs):
+        block, dev = (
+            (w.at[yy, zh], cross),
+            (w.at[yy, near], pair),
+            (w.at[yy, back, half(1 - zl)], cross),
+            (w.at[yy, far, half(zl)], pair),
+        )[phase]
+        send(block, block, ss.at[phase], rs.at[phase], dev)
+
+    def z_wait(w, yy, phase, rs):
+        block = (w.at[yy, near], w.at[yy, back], w.at[yy, far, half(zl)], w.at[yy, far, half(1 - zl)])[phase]
+        arrived(block, rs.at[phase])
+
+    def h_send(r, phase):
+        z_send(w1, (y + r) % 4, phase, hz_s.at[r], hz_r.at[r])
+
+    def h_pass(r, phase):
+        z_wait(w1, (y + r) % 4, phase, hz_r.at[r])
+        if phase < 3:
+            h_send(r, phase + 1)
+
+    def h_first(o):
+        yy = mod4(y - o)
+        arrived(w1.at[yy, zh], hy_r.at[o - 1])
+        h_send(4 - o, 0)
+
+    roles = (
+        (zh, pl.ds(0, 128)), (near, pl.ds(0, 128)), (back, pl.ds(0, 128)), (far, half(zl)), (far, half(1 - zl)),
+    )
+
+    def g_along_y(role):
+        zz, rows = roles[role]
         for o in (1, 3, 2):
-            send(w2.at[y, zz], w2.at[y, zz], gy_s.at[role, o - 1], gy_r.at[role, o - 1], at(dy=o))
-
-    z1(w2, y, gz1_s, gz1_r)
+            send(w2.at[y, zz, rows], w2.at[y, zz, rows], gy_s.at[role, o - 1], gy_r.at[role, o - 1], at(dy=o))
+
+    def g_pass(phase):
+        z_wait(w2, y, phase, gz_r)
+        if phase < 3:
+            z_send(w2, y, phase + 1, gz_s, gz_r)
+        g_along_y(phase + 1)
+
+    z_send(w2, y, 0, gz_s, gz_r)
     for o in (1, 3, 2):
         send(w1.at[y, zh], w1.at[y, zh], hy_s.at[o - 1], hy_r.at[o - 1], at(dy=o))
-    z1(w1, y, hz1_s.at[0], hz1_r.at[0])
-    w2_along_y(zh, 0)
+    h_send(0, 0)
+    g_along_y(0)
 
     def transpose_rows(r):
         for n in range(8):
@@ -136,72 +158,116 @@
     lo, hi = pl.ds(0, 128), pl.ds(128, 128)
     xe, xw, xf = (x + 1) % 4, (x + 3) % 4, (x + 2) % 4
 
-    for i in range(4):
+    def put(ref, i, rows, value):
+        for q in range(4):
+            ref[i, q, rows] = value[:, q * 128 : q * 128 + 128].astype(ref.dtype)
+
+    def get(ref, i, rows):
+        return jnp.concatenate([ref[i, q, rows].astype(F32) for q in range(4)], axis=1)
+
+    top, low = slice(0, 128), slice(128, 256)
+
+    def tokens_of(yy, q):
+        return tk[yy, :, pl.ds(pl.multiple_of(((zh + q + 1) % 4) * 128, 128), 128)]
+
+    def chunk(yy):
+        return jnp.concatenate([tokens_of(yy, q) for q in range(4)], axis=1)
+
+    def s1(i):
         yy = (y + i + 1) % 4
         pltpu.make_async_copy(tk.at[yy, pl.ds(0, 256)], tk.at[yy, pl.ds(0, 256)], tok_l.at[i]).wait()
         arrived(tk.at[yy, pl.ds(256, 256)], tok_r.at[i])
-        s1s[i] = nn(ctt[xf], tk[yy]).astype(BF)
-        send(s1s.at[i, lo], s1r.at[i, lo], s1_s.at[i, 0], s1_q.at[i, 0], east)
-        send(s1s.at[i, hi], s1r.at[i, hi], s1_s.at[i, 1], s1_q.at[i, 1], west)
+        put(s1s, i, slice(0, 256), nn(ctt[xf], chunk(yy)))
+        send(s1s.at[i, :, lo], s1r.at[i, :, lo], s1_s.at[i, 0], s1_q.at[i, 0], east)
+        send(s1s.at[i, :, hi], s1r.at[i, :, hi], s1_s.at[i, 1], s1_q.at[i, 1], west)
+
+    def pieces(i):
+        return ((i, slice(None)),) if i < 3 else tuple((3 + q, q) for q in range(4))
 
     def x_step(i):
-        yy = (y + i + 1) % 4
-        right, left = nn(ctt[xe], tk[yy]), nn(ctt[xw], tk[yy])
-        dps[i, 128:256] = right[128:256].astype(BF)
-        dps[i, 0:128] = left[0:128].astype(BF)
-        send(dps.at[i, hi], dpr.at[i, hi], dp_s.at[i, 1], dp_q.at[i, 1], east)
-        send(dps.at[i, lo], dpr.at[i, lo], dp_s.at[i, 0], dp_q.at[i, 0], west)
-        arrived(s1r.at[i, lo], s1_q.at[i, 0])
-        s2s[i, 0:128] = (right[0:128] + s1r[i, 0:128].astype(F32)).astype(BF)
-        send(s2s.at[i, lo], s2r.at[i, lo], s2_s.at[i, 0], s2_q.at[i, 0], east)
-        arrived(s1r.at[i, hi], s1_q.at[i, 1])
-        s2s[i, 128:256] = (left[128:256] + s1r[i, 128:256].astype(F32)).astype(BF)
-        send(s2s.at[i, hi], s2r.at[i, hi], s2_s.at[i, 1], s2_q.at[i, 1], west)
+        tokens = chunk((y + i + 1) % 4)
+        right, left = nn(ctt[xe], tokens), nn(ctt[xw], tokens)
+        put(dps, i, low, right[128:256])
+        put(dps, i, top, left[0:128])
+        arrived(s1r.at[i, :, lo], s1_q.at[i, 0])
+        put(s2s, i, top, right[0:128] + get(s1r, i, top))
+        arrived(s1r.at[i, :, hi], s1_q.at[i, 1])
+        put(s2s, i, low, left[128:256] + get(s1r, i, low))
+        for k, q in pieces(i):
+            send(s2s.at[i, q, lo], s2r.at[i, q, lo], s2_s.at[k, 0], s2_q.at[k, 0], east)
+            send(s2s.at[i, q, hi], s2r.at[i, q, hi], s2_s.at[k, 1], s2_q.at[k, 1], west)
+            send(dps.at[i, q, hi], dpr.at[i, q, hi], dp_s.at[k, 1], dp_q.at[k, 1], east)
+            send(dps.at[i, q, lo], dpr.at[i, q, lo], dp_s.at[k, 0], dp_q.at[k, 0], west)
+
+    def x_wait(i, k, q):
+        for j, rows in ((0, lo), (1, hi)):
+            arrived(s2r.at[i, q, rows], s2_q.at[k, j])
+            arrived(dpr.at[i, q, rows], dp_q.at[k, j])
 
     def x_end(i):
-        yy = (y + i + 1) % 4
-        total = nn(ctt[x], tk[yy])
-        for k, rows in ((0, lo), (1, hi)):
-            arrived(dpr.at[i, rows], dp_q.at[i, k])
-            arrived(s2r.at[i, rows], s2_q.at[i, k])
-        total = total + dpr[i].astype(F32) + s2r[i].astype(F32)
-        if i < 3:
-            ys[i] = total.astype(BF)
-            send(ys.at[i], yr.at[i], y_s.at[i], y_q.at[i], at(dy=i + 1))
+        total = nn(ctt[x], chunk((y + i + 1) % 4))
+        x_wait(i, i, slice(None))
+        both = slice(0, 256)
+        put(ys, i, both, total + get(dpr, i, both) + get(s2r, i, both))
+        for q in range(4):
+            send(ys.at[i, q], yr.at[i, q], y_s.at[i, q], y_q.at[i, q], at(dy=i + 1))
+
+    def own_chunk():
+        total = nn(ctt[x], chunk(y))
+        for q in range(4):
+            xo[q] = total[:, q * 128 : q * 128 + 128]
+
+    def last(q):
+        total = xo[q]
+        x_wait(3, 3 + q, q)
+        total = total + dpr[3, q].astype(F32) + s2r[3, q].astype(F32)
+        for i in range(3):
+            arrived(yr.at[i, q], y_q.at[i, q])
+            total = total + yr[i, q].astype(F32)
+        zs[q, 0] = total[0:128].astype(BF)
+        zs[q, 1] = total[128:256].astype(BF)
+        if q < 3:
+            for t in range(2):
+                dz = 2 * (q + 1) + t - zl
+                send(zs.at[q, t], zr.at[q * 2 + zl], z_s.at[q * 2 + t], z_q.at[q * 2 + zl], at(dz=dz))
         else:
-            xo[...] = total
-
-    z1_arrived(w2, y, gz1_r)
-    z2(w2, y, gz2_s, gz2_r)
-    w2_along_y(mod4(zh + dirz), 1)
-    for o in (1, 3, 2):
-        yy = mod4(y - o)
-        arrived(w1.at[yy, zh], hy_r.at[o - 1])
-        z1(w1, yy, hz1_s.at[4 - o], hz1_r.at[4 - o])
+            send(zs.at[q, 1 - zl], zr.at[6], z_s.at[6], z_q.at[6], pair)
+            yt[0] = total[0:128]
+            yt[1] = total[128:256]
+
+    for i in range(4):
+        s1(i)
+    g_pass(0)
+    h_first(1)
+    h_first(3)
+    h_pass(0, 0)
     x_step(0)
-    z2_arrived(w2, y, gz2_r)
-    w2_along_y(mod4(zh - dirz), 2)
-    w2_along_y(mod4(zh + 2), 3)
-    z1_arrived(w1, y, hz1_r.at[0])
-    z2(w1, y, hz2_s.at[0], hz2_r.at[0])
+    g_pass(1)
+    h_first(2)
+    h_pass(0, 1)
+    h_pass(3, 0)
+    h_pass(1, 0)
     x_step(1)
-    for o in (1, 3):
-        yy = mod4(y - o)
-        z1_arrived(w1, yy, hz1_r.at[4 - o])
-        z2(w1, yy, hz2_s.at[4 - o], hz2_r.at[4 - o])
+    g_pass(2)
+    h_pass(0, 2)
+    h_pass(3, 1)
+    h_pass(1, 1)
+    h_pass(2, 0)
     x_step(2)
-    yy = mod4(y - 2)
-    z1_arrived(w1, yy, hz1_r.at[2])
-    z2(w1, yy, hz2_s.at[2], hz2_r.at[2])
+    g_pass(3)
+    h_pass(3, 2)
+    h_pass(1, 2)
+    h_pass(2, 1)
     x_step(3)
+    h_pass(2, 2)
     x_end(0)
 
     for r in range(4):
-        z2_arrived(w1, (y + r) % 4, hz2_r.at[r])
-    roles = (zh, mod4(zh + dirz), mod4(zh - dirz), mod4(zh + 2))
-    for role in range(4):
+        h_pass(r, 3)
+    for role in range(5):
+        zz, rows = roles[role]
         for o in (1, 3, 2):
-            arrived(w2.at[mod4(y - o), roles[role]], gy_r.at[role, o - 1])
+            arrived(w2.at[mod4(y - o), zz, rows], gy_r.at[role, o - 1])
 
     def use_weight(p):
         a, b = w1[p].reshape(512, 512), w2[p].reshape(512, 512)
@@ -225,24 +291,16 @@
     use_weight(0)
     x_end(1)
     use_weight(1)
+    use_weight(2)
     x_end(2)
-    use_weight(2)
-    x_end(3)
-    for i in range(3):
-        arrived(yr.at[i], y_q.at[i])
-    total = xo[...] + yr[0].astype(F32) + yr[1].astype(F32) + yr[2].astype(F32)
-    for b in range(8):
-        block = total[(b % 2) * 128 : (b % 2) * 128 + 128, (b // 2) * 128 : (b // 2) * 128 + 128]
-        yt[b] = block
-        zs[b] = block.astype(BF)
-    for j in (4, 3, 5, 2, 6, 1, 7):
-        send(zs.at[(z + j) % 8], zr.at[j - 1], z_s.at[j - 1], z_q.at[j - 1], at(dz=j))
     use_weight(3)
     send(kacc.at[pl.ds(256, 256)], krecv, key_s, key_r, sib)
-    for j in (1, 7, 2, 6, 3, 5, 4):
-        arrived(zr.at[j - 1], z_q.at[j - 1])
-    acc = yt[z]
+    own_chunk()
+    for q in range(4):
+        last(q)
+    acc = yt[zl]
     for j in range(7):
+        arrived(zr.at[j], z_q.at[j])
         acc = acc + zr[j].astype(F32)
     gw_o[...] = jnp.transpose(acc) * 0.00390625
     arrived(krecv, key_r)
@@ -264,21 +322,21 @@
 def shards(tokens, cotangent, quantized, scales):
     dma = pltpu.SemaphoreType.DMA
     vm = pltpu.VMEM
-    piece = (4, 256, 512)
+    piece = (4, 4, 256, 128)
     scratch = [
         vm((4, 512, 512), BF), vm((512, 1024), BF), vm((4, 256, 512), BF),
         vm((4, 4, 128, 512), BF), vm((4, 4, 128, 512), BF),
         vm(piece, BF), vm(piece, BF), vm(piece, BF), vm(piece, BF), vm(piece, BF), vm(piece, BF),
-        vm((256, 512), F32), vm((3, 256, 512), BF), vm((3, 256, 512), BF),
-        vm((8, 128, 128), F32), vm((8, 128, 128), BF), vm((7, 128, 128), BF),
+        vm((4, 256, 128), F32), vm((3, 4, 256, 128), BF), vm((3, 4, 256, 128), BF),
+        vm((2, 128, 128), F32), vm((4, 2, 128, 128), BF), vm((7, 128, 128), BF),
         vm((512, 1024), F32), vm((256, 1024), F32), vm((256, 1024), BF), vm((4, 512, 512), BF),
         dma((4,)), dma((4,)), dma((4,)), dma, dma, dma, dma, dma, dma, dma, dma, dma,
-        dma((3,)), dma((3,)), dma((4, 2)), dma((4, 2)), dma((4, 2)), dma((4, 2)),
-        dma((2,)), dma((2,)), dma((2,)), dma((2,)), dma((4, 3)), dma((4, 3)),
-        dma((4, 2)), dma((4, 2)), dma((4, 2)), dma((4, 2)), dma((4, 2)), dma((4, 2)),
-        dma((3,)), dma((3,)), dma((7,)), dma((7,)),
+        dma((3,)), dma((3,)), dma((4, 4)), dma((4, 4)), dma((4,)), dma((4,)), dma((5, 3)), dma((5, 3)),
+        dma((4, 2)), dma((4, 2)), dma((7, 2)), dma((7, 2)), dma((7, 2)), dma((7, 2)),
+        dma((3, 4)), dma((3, 4)), dma((7,)), dma((7,)),
     ]
     anywhere = pl.BlockSpec(memory_space=pl.ANY)
+    hbm = pl.BlockSpec(memory_space=pltpu.HBM)
     vmem = pl.BlockSpec(memory_space=pltpu.VMEM)
     return pl.pallas_call(
         kernel,
@@ -287,7 +345,7 @@
             jax.ShapeDtypeStruct((256, 4096), BF),
             jax.ShapeDtypeStruct((128, 128), F32),
         ),
-        in_specs=[anywhere, anywhere, vmem, vmem],
+        in_specs=[hbm, hbm, vmem, vmem],
         out_specs=(anywhere, anywhere, vmem),
         scratch_shapes=scratch,
         compiler_params=pltpu.CompilerParams(

time: 76.9 us -> 67.6 us (0.88)
  Pallas kernels: 69.1 us -> 59.7 us
    pallas_call x1, Pallas kernels: 69.1 us -> 59.7 us  [shards(): pl.pallas_call(kernel, out_shape=(jax.ShapeDtypeStruct((256, 1024), BF),...]
where the time goes in v2:
time: 67.6 us; the launch traced here: 67.3 us
  Pallas kernels  59.7 us (88%)
  local copies, waits for them, and re-layouts  7 us (10%)
    pallas_call x1, Pallas kernels, shards(): pl.pallas_call(kernel, out_shape=(jax.ShapeDtypeStruct((256, 1024), BF),...  59.7 us
    unnamed x11, local copies, waits for them, and re-layouts  7 us

profile of v2, /device:TPU:8, one launch (start us, length us, event | category | flops | bytes accessed | tf_op | source)
XLA Modules:
  0.0 67.3 jit_solution(4250792859557501096)
XLA Ops:
  0.6 0.0 copy-start
  0.6 1.6 %copy-done = bf16[256,4096]{1,0:T(8,128)(2,1)S(1)} copy-done((bf16[256,4096]{1,0:T(8,128)(2,1)S(1)}, bf16[256,4096]{1,0:T(8,128)(2,1)}, u32[]{:S(2)}) %copy-start) | copy-done | bytes 2097176
  2.2 0.0 copy-start.1
  2.2 1.0 %copy-done.1 = bf16[256,1024]{1,0:T(8,128)(2,1)S(1)} copy-done((bf16[256,1024]{1,0:T(8,128)(2,1)S(1)}, bf16[256,1024]{1,0:T(8,128)(2,1)}, u32[]{:S(2)}) %copy-start.1) | copy-done | bytes 524312
  3.3 0.0 copy-start.2
  3.3 0.9 %copy-done.2 = bf16[128,1024]{1,0:T(8,128)(2,1)S(1)} copy-done((bf16[128,1024]{1,0:T(8,128)(2,1)S(1)}, bf16[128,1024]{1,0:T(8,128)(2,1)}, u32[]{:S(2)}) %copy-start.2) | copy-done | bytes 262168
  4.2 0.0 copy-start.3
  4.2 0.7 %copy-done.3 = f32[128,4]{0,1:T(4,128)S(1)} copy-done((f32[128,4]{0,1:T(4,128)S(1)}, f32[128,4]{0,1:T(4,128)}, u32[]{:S(2)}) %copy-start.3) | copy-done | bytes 2072
  4.9 59.7 %key_projection.1 = (bf16[256,1024]{1,0:T(8,128)(2,1)S(1)}, bf16[256,4096]{1,0:T(8,128)(2,1)S(1)}, f32[128,128]{1,0:T(8,128)S(1)}) custom-call(bf16[256,4096]{1,0:T(8,128)(2,1)S(1)} %copy-done, bf16[256,1024]{1,0:T(8,128)(2,1)S(1)} %copy-done.1, bf16[128,1024]{1,0:T(8,128)(2,1)S(1)} %copy-done.2, f32[4,128]{1,0:T(4,128)S(1)} %bitcast.1), custom_call_target="tpu_custom_call" | custom-call | flops 6442450944 | bytes 8388608 | tf_op jit(solution)/shard_map/key_projection/pallas_call | solution.py:341
  64.6 0.8 %copy.10 = bf16[256,1024]{1,0:T(8,128)(2,1)} copy(bf16[256,1024]{1,0:T(8,128)(2,1)S(1)} %get-tuple-element.6) | data formatting | bytes 1048576
  65.4 1.3 %copy.11 = bf16[256,4096]{1,0:T(8,128)(2,1)} copy(bf16[256,4096]{1,0:T(8,128)(2,1)S(1)} %get-tuple-element.7) | data formatting | bytes 4194304
  66.7 0.6 copy.12
Async XLA Ops:
  0.6 1.6 %copy-start = (bf16[256,4096]{1,0:T(8,128)(2,1)S(1)}, bf16[256,4096]{1,0:T(8,128)(2,1)}, u32[]{:S(2)}) copy-start(bf16[256,4096]{1,0:T(8,128)(2,1)} %tok.1) | copy-start | bytes 6291460
  2.2 1.0 %copy-start.1 = (bf16[256,1024]{1,0:T(8,128)(2,1)S(1)}, bf16[256,1024]{1,0:T(8,128)(2,1)}, u32[]{:S(2)}) copy-start(bf16[256,1024]{1,0:T(8,128)(2,1)} %cot.1) | copy-start | bytes 1572868
  3.3 0.9 %copy-start.2 = (bf16[128,1024]{1,0:T(8,128)(2,1)S(1)}, bf16[128,1024]{1,0:T(8,128)(2,1)}, u32[]{:S(2)}) copy-start(bf16[128,1024]{1,0:T(8,128)(2,1)} %quantized.1) | copy-start | bytes 786436
  4.2 0.7 %copy-start.3 = (f32[128,4]{0,1:T(4,128)S(1)}, f32[128,4]{0,1:T(4,128)}, u32[]{:S(2)}) copy-start(f32[128,4]{0,1:T(4,128)} %param.7) | copy-start | bytes 6148

commit v3 on v2

--- a/solution.py
+++ b/solution.py
@@ -19,9 +19,9 @@
 
 
 def kernel(
-    tok, cot, quantized, scales_t, keys_o, gi_o, gw_o,
-    tk, ct, ctt, w1, w2, s1s, s1r, dps, dpr, s2s, s2r, xo, ys, yr, yt, zs, zr, kacc, krecv, kout, gis,
-    tok_l, tok_s, tok_r, cot_l, cot_s, cot_r, key_s, key_r, key_l, gi_l, gi_s, gi_r,
+    tok, cot, codes_h, scales_h, keys_o, gi_o, gw_o,
+    quantized, scales_t, tk, ct, ctt, w1, w2, s1s, s1r, dps, dpr, s2s, s2r, xo, ys, yr, yt, zs, zr, kacc, krecv, kout, gis,
+    codes_l, scales_l, tok_l, tok_s, tok_r, cot_l, cot_s, cot_r, key_s, key_r, key_l, gi_l, gi_s, gi_r,
     hy_s, hy_r, hz_s, hz_r, gz_s, gz_r, gy_s, gy_r,
     s1_s, s1_q, dp_s, dp_q, s2_s, s2_q, y_s, y_q, z_s, z_q,
 ):
@@ -50,6 +50,11 @@
     def mod4(v):
         return (v + 4) % 4
 
+    barrier = pltpu.get_barrier_semaphore()
+    peers = [at(dx=1), at(dx=-1)] + [at(dy=o) for o in (1, 2, 3)] + [at(dz=j) for j in range(1, 8)] + [sib]
+    for peer in peers:
+        pl.semaphore_signal(barrier, inc=1, device_id=peer, device_id_type=MESH)
+
     def cols(yy, h):
         return pl.ds(pl.multiple_of(((yy * 4 + h) * 2 + c) * 128, 128), 128)
 
@@ -58,6 +63,10 @@
 
     cp_cot = pltpu.make_async_copy(cot, ct.at[pl.ds(0, 256)], cot_l)
     cp_cot.start()
+    cp_scales = pltpu.make_async_copy(scales_h, scales_t, scales_l)
+    cp_scales.start()
+    cp_codes = pltpu.make_async_copy(codes_h, quantized, codes_l)
+    cp_codes.start()
     for i in range(4):
         yy = (y + i + 1) % 4
         for h in range(4):
@@ -65,6 +74,8 @@
                 tok.at[:, cols(yy, h)], tk.at[yy, pl.ds(0, 256), pl.ds(h * 128, 128)], tok_l.at[i]
             ).start()
 
+    cp_scales.wait()
+    cp_codes.wait()
     for b in range(4):
         scale = jnp.transpose(jnp.broadcast_to(scales_t[b : b + 1, :], (128, 128)))
         for half in range(2):
@@ -75,10 +86,6 @@
             else:
                 w2[y, zh, :, col - 512 : col - 384] = block
 
-    barrier = pltpu.get_barrier_semaphore()
-    peers = [at(dx=1), at(dx=-1)] + [at(dy=o) for o in (1, 2, 3)] + [at(dz=j) for j in range(1, 8)] + [sib]
-    for peer in peers:
-        pl.semaphore_signal(barrier, inc=1, device_id=peer, device_id_type=MESH)
     pl.semaphore_wait(barrier, len(peers))
 
     send(cot, ct.at[pl.ds(256, 256)], cot_s, cot_r, sib)
@@ -182,7 +189,7 @@
         send(s1s.at[i, :, hi], s1r.at[i, :, hi], s1_s.at[i, 1], s1_q.at[i, 1], west)
 
     def pieces(i):
-        return ((i, slice(None)),) if i < 3 else tuple((3 + q, q) for q in range(4))
+        return ((i, slice(None)),) if i < 2 else tuple((4 * i - 6 + q, q) for q in range(4))
 
     def x_step(i):
         tokens = chunk((y + i + 1) % 4)
@@ -206,10 +213,13 @@
 
     def x_end(i):
         total = nn(ctt[x], chunk((y + i + 1) % 4))
-        x_wait(i, i, slice(None))
-        both = slice(0, 256)
-        put(ys, i, both, total + get(dpr, i, both) + get(s2r, i, both))
+        if i < 2:
+            x_wait(i, i, slice(None))
         for q in range(4):
+            if i == 2:
+                x_wait(i, 2 + q, q)
+            piece = total[:, q * 128 : q * 128 + 128]
+            ys[i, q] = (piece + dpr[i, q].astype(F32) + s2r[i, q].astype(F32)).astype(BF)
             send(ys.at[i, q], yr.at[i, q], y_s.at[i, q], y_q.at[i, q], at(dy=i + 1))
 
     def own_chunk():
@@ -219,7 +229,7 @@
 
     def last(q):
         total = xo[q]
-        x_wait(3, 3 + q, q)
+        x_wait(3, 6 + q, q)
         total = total + dpr[3, q].astype(F32) + s2r[3, q].astype(F32)
         for i in range(3):
             arrived(yr.at[i, q], y_q.at[i, q])
@@ -261,6 +271,7 @@
     x_step(3)
     h_pass(2, 2)
     x_end(0)
+    x_end(1)
 
     for r in range(4):
         h_pass(r, 3)
@@ -289,10 +300,9 @@
             kacc[:, 512:1024] += nn(tk[p], b)
 
     use_weight(0)
-    x_end(1)
     use_weight(1)
+    x_end(2)
     use_weight(2)
-    x_end(2)
     use_weight(3)
     send(kacc.at[pl.ds(256, 256)], krecv, key_s, key_r, sib)
     own_chunk()
@@ -324,15 +334,15 @@
     vm = pltpu.VMEM
     piece = (4, 4, 256, 128)
     scratch = [
-        vm((4, 512, 512), BF), vm((512, 1024), BF), vm((4, 256, 512), BF),
+        vm((128, 1024), BF), vm((4, 128), F32), vm((4, 512, 512), BF), vm((512, 1024), BF), vm((4, 256, 512), BF),
         vm((4, 4, 128, 512), BF), vm((4, 4, 128, 512), BF),
         vm(piece, BF), vm(piece, BF), vm(piece, BF), vm(piece, BF), vm(piece, BF), vm(piece, BF),
         vm((4, 256, 128), F32), vm((3, 4, 256, 128), BF), vm((3, 4, 256, 128), BF),
         vm((2, 128, 128), F32), vm((4, 2, 128, 128), BF), vm((7, 128, 128), BF),
         vm((512, 1024), F32), vm((256, 1024), F32), vm((256, 1024), BF), vm((4, 512, 512), BF),
-        dma((4,)), dma((4,)), dma((4,)), dma, dma, dma, dma, dma, dma, dma, dma, dma,
+        dma, dma, dma((4,)), dma((4,)), dma((4,)), dma, dma, dma, dma, dma, dma, dma, dma, dma,
         dma((3,)), dma((3,)), dma((4, 4)), dma((4, 4)), dma((4,)), dma((4,)), dma((5, 3)), dma((5, 3)),
-        dma((4, 2)), dma((4, 2)), dma((7, 2)), dma((7, 2)), dma((7, 2)), dma((7, 2)),
+        dma((4, 2)), dma((4, 2)), dma((10, 2)), dma((10, 2)), dma((10, 2)), dma((10, 2)),
         dma((3, 4)), dma((3, 4)), dma((7,)), dma((7,)),
     ]
     anywhere = pl.BlockSpec(memory_space=pl.ANY)
@@ -345,7 +355,7 @@
             jax.ShapeDtypeStruct((256, 4096), BF),
             jax.ShapeDtypeStruct((128, 128), F32),
         ),
-        in_specs=[hbm, hbm, vmem, vmem],
+        in_specs=[hbm] * 4,
         out_specs=(anywhere, anywhere, vmem),
         scratch_shapes=scratch,
         compiler_params=pltpu.CompilerParams(
@@ -353,7 +363,7 @@
         ),
         cost_estimate=pl.CostEstimate(flops=6442450944, bytes_accessed=8 * 2**20, transcendentals=0),
         name="key_projection",
-    )(tokens, cotangent, quantized, scales.T)
+    )(*(pltpu.with_memory_space_constraint(v, pltpu.HBM) for v in (tokens, cotangent, quantized, scales.T)))
 
 
 def solution(mesh):

time: 67.6 us -> 61 us (0.902)
  local copies, waits for them, and re-layouts: 7 us -> 2.74 us
  Pallas kernels: 59.7 us -> 57.5 us
    unnamed x11 -> x3, local copies, waits for them, and re-layouts: 7 us -> 2.74 us
    pallas_call x1, Pallas kernels: 59.7 us -> 57.5 us  [shards(): pl.pallas_call(kernel, out_shape=(jax.ShapeDtypeStruct((256, 1024), BF),...]
where the time goes in v3:
time: 61 us; the launch traced here: 60.9 us
  Pallas kernels  57.5 us (94%)
  local copies, waits for them, and re-layouts  2.74 us (4%)
  between operations  0.64 us (1%)
    pallas_call x1, Pallas kernels, shards(): pl.pallas_call(kernel, out_shape=(jax.ShapeDtypeStruct((256, 1024), BF),...  57.5 us
    unnamed x3, local copies, waits for them, and re-layouts  2.74 us

profile of v3, /device:TPU:8, one launch (start us, length us, event | category | flops | bytes accessed | tf_op | source)
XLA Modules:
  0.0 60.9 jit_solution(6415515225374893533)
XLA Ops:
  0.6 57.5 %key_projection.1 = (bf16[256,1024]{1,0:T(8,128)(2,1)S(1)}, bf16[256,4096]{1,0:T(8,128)(2,1)S(1)}, f32[128,128]{1,0:T(8,128)S(1)}) custom-call(bf16[256,4096]{1,0:T(8,128)(2,1)} %tok.1, bf16[256,1024]{1,0:T(8,128)(2,1)} %cot.1, bf16[128,1024]{1,0:T(8,128)(2,1)} %codes_h.1, f32[4,128]{1,0:T(4,128)} %bitcast.1), custom_call_target="tpu_custom_call" | custom-call | flops 6442450944 | bytes 8388608 | tf_op jit(solution)/shard_map/key_projection/pallas_call | solution.py:351
  58.1 0.8 %copy.10 = bf16[256,1024]{1,0:T(8,128)(2,1)} copy(bf16[256,1024]{1,0:T(8,128)(2,1)S(1)} %get-tuple-element.6) | data formatting | bytes 1048576
  58.9 1.3 %copy.11 = bf16[256,4096]{1,0:T(8,128)(2,1)} copy(bf16[256,4096]{1,0:T(8,128)(2,1)S(1)} %get-tuple-element.7) | data formatting | bytes 4194304
  60.2 0.6 %copy.12 = f32[128,128]{1,0:T(8,128)} copy(f32[128,128]{1,0:T(8,128)S(1)} %get-tuple-element.8) | data formatting | bytes 131072

commit v4 on v3

--- a/solution.py
+++ b/solution.py
@@ -71,7 +71,18 @@
         yy = (y + i + 1) % 4
         for h in range(4):
             pltpu.make_async_copy(
-                tok.at[:, cols(yy, h)], tk.at[yy, pl.ds(0, 256), pl.ds(h * 128, 128)], tok_l.at[i]
+                tok.at[:, cols(yy, h)], tk.at[yy, h, pl.ds(0, 256)], tok_l.at[i]
+            ).start()
+
+    pl.semaphore_wait(barrier, len(peers))
+
+    send(cot, ct.at[pl.ds(256, 256)], cot_s, cot_r, sib)
+    for i in range(4):
+        yy = (y + i + 1) % 4
+        for h in range(4):
+            pltpu.make_async_remote_copy(
+                tok.at[:, cols_sib(yy, h)], tk.at[yy, h, pl.ds(256, 256)],
+                tok_s.at[i], tok_r.at[i], device_id=sib, device_id_type=MESH,
             ).start()
 
     cp_scales.wait()
@@ -86,17 +97,6 @@
             else:
                 w2[y, zh, :, col - 512 : col - 384] = block
 
-    pl.semaphore_wait(barrier, len(peers))
-
-    send(cot, ct.at[pl.ds(256, 256)], cot_s, cot_r, sib)
-    for i in range(4):
-        yy = (y + i + 1) % 4
-        for h in range(4):
-            pltpu.make_async_remote_copy(
-                tok.at[:, cols_sib(yy, h)], tk.at[yy, pl.ds(256, 256), pl.ds(h * 128, 128)],
-                tok_s.at[i], tok_r.at[i], device_id=sib, device_id_type=MESH,
-            ).start()
-
     def half(flag):
         return pl.ds(pl.multiple_of(flag * 64, 64), 64)
 
@@ -174,16 +174,18 @@
 
     top, low = slice(0, 128), slice(128, 256)
 
+    order = (2, 1, 3, 0)
+
     def tokens_of(yy, q):
-        return tk[yy, :, pl.ds(pl.multiple_of(((zh + q + 1) % 4) * 128, 128), 128)]
+        return tk[yy, (zh + order[q]) % 4]
 
     def chunk(yy):
         return jnp.concatenate([tokens_of(yy, q) for q in range(4)], axis=1)
 
     def s1(i):
         yy = (y + i + 1) % 4
-        pltpu.make_async_copy(tk.at[yy, pl.ds(0, 256)], tk.at[yy, pl.ds(0, 256)], tok_l.at[i]).wait()
-        arrived(tk.at[yy, pl.ds(256, 256)], tok_r.at[i])
+        pltpu.make_async_copy(tk.at[yy, :, pl.ds(0, 256)], tk.at[yy, :, pl.ds(0, 256)], tok_l.at[i]).wait()
+        arrived(tk.at[yy, :, pl.ds(256, 256)], tok_r.at[i])
         put(s1s, i, slice(0, 256), nn(ctt[xf], chunk(yy)))
         send(s1s.at[i, :, lo], s1r.at[i, :, lo], s1_s.at[i, 0], s1_q.at[i, 0], east)
         send(s1s.at[i, :, hi], s1r.at[i, :, hi], s1_s.at[i, 1], s1_q.at[i, 1], west)
@@ -238,22 +240,44 @@
         zs[q, 1] = total[128:256].astype(BF)
         if q < 3:
             for t in range(2):
-                dz = 2 * (q + 1) + t - zl
+                dz = 2 * order[q] + t - zl
                 send(zs.at[q, t], zr.at[q * 2 + zl], z_s.at[q * 2 + t], z_q.at[q * 2 + zl], at(dz=dz))
         else:
             send(zs.at[q, 1 - zl], zr.at[6], z_s.at[6], z_q.at[6], pair)
             yt[0] = total[0:128]
             yt[1] = total[128:256]
 
-    for i in range(4):
-        s1(i)
+    def use_weight(p):
+        tokens = jnp.concatenate([tk[p, h] for h in range(4)], axis=1)
+        a, b = w1[p].reshape(512, 512), w2[p].reshape(512, 512)
+        for r in range(2):
+            rows = slice(r * 256, r * 256 + 256)
+            gis[p, rows] = (nt(ct[rows, 0:512], a) + nt(ct[rows, 512:1024], b)).astype(BF)
+        for h in range(4):
+            here = pl.ds(h * 128, 128)
+            pltpu.make_async_remote_copy(
+                gis.at[p, pl.ds(256, 256), here], gi_o.at[:, cols(p, h)],
+                gi_s, gi_r, device_id=sib, device_id_type=MESH,
+            ).start()
+            pltpu.make_async_copy(gis.at[p, pl.ds(0, 256), here], gi_o.at[:, cols(p, h)], gi_l).start()
+        if p == 0:
+            kacc[:, 0:512] = nn(tokens, a)
+            kacc[:, 512:1024] = nn(tokens, b)
+        else:
+            kacc[:, 0:512] += nn(tokens, a)
+            kacc[:, 512:1024] += nn(tokens, b)
+
+    s1(0)
+    s1(1)
     g_pass(0)
     h_first(1)
     h_first(3)
     h_pass(0, 0)
-    x_step(0)
+    s1(2)
+    s1(3)
     g_pass(1)
     h_first(2)
+    x_step(0)
     h_pass(0, 1)
     h_pass(3, 0)
     h_pass(1, 0)
@@ -268,37 +292,19 @@
     h_pass(3, 2)
     h_pass(1, 2)
     h_pass(2, 1)
+    early = len(pending)
     x_step(3)
     h_pass(2, 2)
     x_end(0)
     x_end(1)
-
-    for r in range(4):
-        h_pass(r, 3)
+    h_pass(0, 3)
+    h_pass(3, 3)
+    h_pass(1, 3)
+    h_pass(2, 3)
     for role in range(5):
         zz, rows = roles[role]
         for o in (1, 3, 2):
             arrived(w2.at[mod4(y - o), zz, rows], gy_r.at[role, o - 1])
-
-    def use_weight(p):
-        a, b = w1[p].reshape(512, 512), w2[p].reshape(512, 512)
-        for r in range(2):
-            rows = slice(r * 256, r * 256 + 256)
-            gis[p, rows] = (nt(ct[rows, 0:512], a) + nt(ct[rows, 512:1024], b)).astype(BF)
-        for h in range(4):
-            here = pl.ds(h * 128, 128)
-            pltpu.make_async_remote_copy(
-                gis.at[p, pl.ds(256, 256), here], gi_o.at[:, cols(p, h)],
-                gi_s, gi_r, device_id=sib, device_id_type=MESH,
-            ).start()
-            pltpu.make_async_copy(gis.at[p, pl.ds(0, 256), here], gi_o.at[:, cols(p, h)], gi_l).start()
-        if p == 0:
-            kacc[:, 0:512] = nn(tk[p], a)
-            kacc[:, 512:1024] = nn(tk[p], b)
-        else:
-            kacc[:, 0:512] += nn(tk[p], a)
-            kacc[:, 512:1024] += nn(tk[p], b)
-
     use_weight(0)
     use_weight(1)
     x_end(2)
@@ -306,22 +312,24 @@
     use_weight(3)
     send(kacc.at[pl.ds(256, 256)], krecv, key_s, key_r, sib)
     own_chunk()
+    for cp in pending[:early]:
+        cp.wait_send()
+    for i in range(4):
+        pltpu.make_async_copy(tk.at[0, :, pl.ds(256, 256)], tk.at[0, :, pl.ds(256, 256)], tok_s.at[i]).wait()
     for q in range(4):
         last(q)
+    arrived(krecv, key_r)
+    kout[...] = (kacc[0:256] + krecv[...]).astype(BF)
+    cp_key = pltpu.make_async_copy(kout, keys_o, key_l)
+    cp_key.start()
     acc = yt[zl]
     for j in range(7):
         arrived(zr.at[j], z_q.at[j])
         acc = acc + zr[j].astype(F32)
     gw_o[...] = jnp.transpose(acc) * 0.00390625
-    arrived(krecv, key_r)
-    kout[...] = (kacc[0:256] + krecv[...]).astype(BF)
-    cp_key = pltpu.make_async_copy(kout, keys_o, key_l)
-    cp_key.start()
-
-    for cp in pending:
+
+    for cp in pending[early:]:
         cp.wait_send()
-    for i in range(4):
-        pltpu.make_async_copy(tk.at[0, pl.ds(256, 256)], tk.at[0, pl.ds(256, 256)], tok_s.at[i]).wait()
     wide = pl.ds(0, 2048)
     pltpu.make_async_copy(gi_o.at[:, wide], gi_o.at[:, wide], gi_l).wait()
     pltpu.make_async_copy(gi_o.at[:, wide], gi_o.at[:, wide], gi_s).wait()
@@ -334,7 +342,7 @@
     vm = pltpu.VMEM
     piece = (4, 4, 256, 128)
     scratch = [
-        vm((128, 1024), BF), vm((4, 128), F32), vm((4, 512, 512), BF), vm((512, 1024), BF), vm((4, 256, 512), BF),
+        vm((128, 1024), BF), vm((4, 128), F32), vm((4, 4, 512, 128), BF), vm((512, 1024), BF), vm((4, 256, 512), BF),
         vm((4, 4, 128, 512), BF), vm((4, 4, 128, 512), BF),
         vm(piece, BF), vm(piece, BF), vm(piece, BF), vm(piece, BF), vm(piece, BF), vm(piece, BF),
         vm((4, 256, 128), F32), vm((3, 4, 256, 128), BF), vm((3, 4, 256, 128), BF),

time: 61 us -> 60.2 us (0.987)
  Pallas kernels: 57.5 us -> 56.1 us
    pallas_call x1, Pallas kernels: 57.5 us -> 56.1 us  [shards(): pl.pallas_call(kernel, out_shape=(jax.ShapeDtypeStruct((256, 1024), BF),...]
where the time goes in v4:
time: 60.2 us; the launch traced here: 59.5 us
  Pallas kernels  56.1 us (93%)
  local copies, waits for them, and re-layouts  2.74 us (5%)
  between operations  0.64 us (1%)
    pallas_call x1, Pallas kernels, shards(): pl.pallas_call(kernel, out_shape=(jax.ShapeDtypeStruct((256, 1024), BF),...  56.1 us
    unnamed x3, local copies, waits for them, and re-layouts  2.74 us

profile of v4, /device:TPU:8, one launch (start us, length us, event | category | flops | bytes accessed | tf_op | source)
XLA Modules:
  0.0 59.5 jit_solution(3279310166220265185)
XLA Ops:
  0.6 56.1 %key_projection.1 = (bf16[256,1024]{1,0:T(8,128)(2,1)S(1)}, bf16[256,4096]{1,0:T(8,128)(2,1)S(1)}, f32[128,128]{1,0:T(8,128)S(1)}) custom-call(bf16[256,4096]{1,0:T(8,128)(2,1)} %tok.1, bf16[256,1024]{1,0:T(8,128)(2,1)} %cot.1, bf16[128,1024]{1,0:T(8,128)(2,1)} %codes_h.1, f32[4,128]{1,0:T(4,128)} %bitcast.1), custom_call_target="tpu_custom_call" | custom-call | flops 6442450944 | bytes 8388608 | tf_op jit(solution)/shard_map/key_projection/pallas_call | solution.py:359
  56.8 0.8 %copy.10 = bf16[256,1024]{1,0:T(8,128)(2,1)} copy(bf16[256,1024]{1,0:T(8,128)(2,1)S(1)} %get-tuple-element.6) | data formatting | bytes 1048576
  57.6 1.3 %copy.11 = bf16[256,4096]{1,0:T(8,128)(2,1)} copy(bf16[256,4096]{1,0:T(8,128)(2,1)S(1)} %get-tuple-element.7) | data formatting | bytes 4194304
  58.9 0.6 %copy.12 = f32[128,128]{1,0:T(8,128)} copy(f32[128,128]{1,0:T(8,128)S(1)} %get-tuple-element.8) | data formatting | bytes 131072
